TPU v7x, 32 devices: a whole 2x2x4 slice. The times are simulated.
32 devices in a mesh: groups: 2 (over x), ckpt: 4 (over z), wide: 4 (over y, core).
Axes of the slice: x: 2, y: 2, z: 4, core: 2. Of those that a mesh axis runs over, the one named last changes fastest.
Arguments:
- query_grads: bfloat16 [4, 128, 32768], P('ckpt', 'groups', 'wide'), parts along dimension 1, may hold values from -6 to 6
- train_grads: bfloat16 [4, 512, 32768], P('ckpt', 'groups', 'wide'), parts along dimension 1, may hold values from -0.0059814453 to 0.0059814453
- step_rates: float32 [4], P('ckpt'), may hold values from 0.25 to 2
- layer_mask: int32 [4, 4, 4], P('wide'), may hold values from 0 to 1
- train_ids: int32 [256], replicated, may hold values from 0 to 255, each once
Outputs:
- influence: float32 [128, 256], P(('groups', 'ckpt', 'wide')), parts along dimension 0
There are 2 independent parts, one for each index of `groups`. A program takes and returns all parts, laid end to end along the dimension named above; an argument that names none is the same for every part. Nothing has to cross between parts.
Inputs may be any that keep to these rules, and one draw needn't show every extreme that they name: `train_ids`: each stored row once.
All inputs are finite; a program needn't handle non-finite values.
Results may differ from a plain program's by a relative error of at most 0.0003.
Values sent between devices are 32-bit elements; how exact they have to be, the bound alone decides.
A program may use at most 64 MiB of HBM per device.

v0:
```python
import jax
import jax.numpy as jnp
from jax import lax
from jax.sharding import PartitionSpec as P

NQB = 4
NPAN = 4


def shards(query_grads, train_grads, step_rates, layer_mask, train_ids):
    queries = query_grads[0]
    trained = train_grads[0]
    total_rows = queries.shape[0]
    total_cols = trained.shape[0]
    qblock = total_rows // NQB
    panel = total_cols // NPAN
    rate = step_rates[0]
    row_blocks = jnp.arange(total_rows, dtype=jnp.int32) // qblock
    one_hot = (row_blocks[:, None] == jnp.arange(NQB, dtype=jnp.int32)[None, :]).astype(jnp.float32)
    product = lax.dot_general(
        queries, trained, (((1,), (1,)), ((), ())), preferred_element_type=jnp.float32
    )
    product = jnp.take(product, train_ids, axis=1)
    column_mask = jnp.repeat(layer_mask[0].astype(jnp.float32), panel, axis=1)
    weights = jnp.dot(one_hot, column_mask, preferred_element_type=jnp.float32)
    summed = weights * product
    full_term = rate * summed
    influence = lax.psum_scatter(full_term, ("ckpt", "wide"), scatter_dimension=0, tiled=True)
    return influence


def solution(mesh):
    in_specs = (
        P("ckpt", "groups", "wide"),
        P("ckpt", "groups", "wide"),
        P("ckpt"),
        P("wide", None, None),
        P(),
    )
    out_specs = P(("groups", "ckpt", "wide"), None)
    return jax.shard_map(shards, mesh=mesh, in_specs=in_specs, out_specs=out_specs, check_vma=False)
```

profile of v0, /device:TPU:0, one launch (start us, length us, event | category | flops | bytes accessed | tf_op | source)
XLA Modules:
  0.0 109.4 jit_solution(9061899878991760140)
XLA Ops:
  6.5 0.0 copy-start
  6.5 0.0 copy-start.2
  6.5 0.0 copy-start.1
  6.5 0.0 all-reduce.3.cloned.1.call-start
  6.6 0.8 compare_select_fusion
  7.3 0.7 compare_and_fusion
  8.0 0.0 copy-done
  8.0 3.4 %fusion = f32[64,256]{0,1:T(8,128)S(1)} fusion(bf16[1,256,8192]{2,1,0:T(8,128)(2,1)} %param.6, bf16[1,64,8192]{2,1,0:T(8,128)(2,1)S(1)} %copy-done), kind=kOutput, calls=%fused_computation.1 | convolution fusion | flops 268435456 | bytes 5308416 | tf_op jit(solution)/shard_map/dot_general | solution.py:20
  11.5 0.7 gather_fusion
  12.2 0.1 copy.9
  12.3 0.0 copy-done.1
  12.3 0.1 broadcast_in_dim.17
  12.4 0.1 reshape.22
  13.1 0.8 fusion.2
  13.9 0.0 all-reduce.3.cloned.1.call-update
  13.9 0.0 copy-done.2
  14.0 0.6 dynamic-slice
  15.2 86.1 %all-reduce.3.cloned.1.call-done = f32[64,256]{1,0:T(8,128)} async-done(((f32[64,256]{1,0:T(8,128)}), f32[64,256]{1,0:T(8,128)}) %all-reduce.3.cloned.1.call-update) | async-done | bytes 65552
  101.2 1.3 %constant_dynamic-slice_fusion = f32[4,256]{1,0:T(4,128)} fusion(f32[64,256]{1,0:T(8,128)} %all-reduce.3.cloned.1.call-done, u32[]{:T(128)S(6)} %multiply.1), kind=kLoop, calls=%fused_computation.16 | loop fusion | bytes 8196
  (3 shorter events, 0.0 us)
Async XLA Ops:
  6.5 1.5 %copy-start = (bf16[1,64,8192]{2,1,0:T(8,128)(2,1)S(1)}, bf16[1,64,8192]{2,1,0:T(8,128)(2,1)}, u32[]{:S(2)}) copy-start(bf16[1,64,8192]{2,1,0:T(8,128)(2,1)} %param.5) | copy-start | bytes 3145732
  6.5 7.4 %copy-start.2 = (u32[32]{0:T(128)S(1)}, u32[32]{0:T(128)}, u32[]{:S(2)}) copy-start(u32[32]{0:T(128)} %constant.39) | copy-start | bytes 388
  6.5 5.7 %copy-start.1 = (s32[1,4,4]{2,1,0:T(4,128)S(1)}, s32[1,4,4]{2,1,0:T(4,128)}, u32[]{:S(2)}) copy-start(s32[1,4,4]{2,1,0:T(4,128)} %param.8) | copy-start | bytes 196
  6.5 94.7 %all-reduce.3.cloned.1.call-start = ((), (), s32[]{:S(2)}) async-start(), calls=%async_computation | async-start | bytes 131072
Sparse Core Ops, SparseCore 0:
  14.1 87.1 all-reduce.2
where the time goes:
time: 111 us; the launch traced here: 109 us
  waiting for transfers between devices  86.1 us (78%)
  between operations  14.8 us (13%)
  matrix products  4.23 us (4%)
  local copies, waits for them, and re-layouts  2.86 us (3%)
  other arithmetic  1.47 us (1%)
    unnamed x2, waiting for transfers between devices  86.1 us
    dot_general x1, matrix products, shards(): lax.dot_general(queries, trained, (((1,), (1,)), ((), ())), preferred_ele...  3.41 us
  transfers between devices with their start and end apart: 1, of which 1 were waited for; matrix products, arithmetic and copies ran while one was open for 1% of the time, Pallas kernels for 0%

commit v1 on v0

v1 whole, which is shorter than its diff:
```python
import functools

import jax
import jax.numpy as jnp
from jax import lax
from jax.experimental import pallas as pl
from jax.experimental.pallas import tpu as pltpu
from jax.sharding import PartitionSpec as P

NQB = 4
NPAN = 4
LANES = 128
KPARTS = 4
MESH = pl.DeviceIdType.MESH
DIMS = (((1,), (1,)), ((), ()))


def kernel(
    ckpts, wides,
    rate_hbm, mask_hbm, ids_hbm, q_hbm, t_hbm, out_ref,
    rate_ref, mask_ref, ids_ref, q_buf, t_buf, weights, sbuf, rbuf,
    s_sem, q_sem, t_sem, send_sem, recv_sem,
):
    n = ckpts * wides
    rows, depth = q_buf.shape
    cols = t_buf.shape[0]
    halves = cols // LANES
    own = rows // n
    step = depth // KPARTS
    group = lax.axis_index("groups")
    me = lax.axis_index("ckpt") * wides + lax.axis_index("wide")

    def q_copy(k):
        part = pl.ds(k * step, step)
        return pltpu.make_async_copy(q_hbm.at[0, :, part], q_buf.at[:, part], q_sem.at[k])

    def t_copy(h, k):
        part = pl.ds(k * step, step)
        some = pl.ds(h * LANES, LANES)
        return pltpu.make_async_copy(
            t_hbm.at[0, some, part], t_buf.at[some, part], t_sem.at[h, k]
        )

    small = [
        pltpu.make_async_copy(rate_hbm, rate_ref, s_sem.at[0]),
        pltpu.make_async_copy(mask_hbm, mask_ref, s_sem.at[1]),
        pltpu.make_async_copy(ids_hbm, ids_ref, s_sem.at[2]),
    ]
    for copy in small:
        copy.start()
    for h in range(halves):
        for k in range(KPARTS):
            if h == 0:
                q_copy(k).start()
            t_copy(h, k).start()

    def peer(r):
        where = lax.rem(me + r, n)
        return where, (group, where // wides, lax.rem(where, wides))

    barrier = pltpu.get_barrier_semaphore()
    for r in range(1, n):
        pl.semaphore_signal(barrier, inc=1, device_id=peer(r)[1], device_id_type=MESH)

    for copy in small:
        copy.wait()
    ids = ids_ref[...]
    hot = (lax.broadcasted_iota(jnp.int32, (cols, cols), 0) == ids).astype(jnp.bfloat16)
    panel = cols // NPAN
    in_panel = (
        lax.broadcasted_iota(jnp.int32, (16, cols), 1) // panel
        == lax.broadcasted_iota(jnp.int32, (16, cols), 0)
    ).astype(jnp.bfloat16)
    stored = lax.dot_general(in_panel, hot, DIMS, preferred_element_type=jnp.float32)
    qblock = rows // NQB
    rate = rate_ref[0]
    for b in range(NQB):
        row = sum(
            (rate * mask_ref[0, b, p].astype(jnp.float32)) * stored[p : p + 1, :]
            for p in range(NPAN)
        )
        weights[b * qblock : (b + 1) * qblock, :] = jnp.broadcast_to(row, (qblock, cols))

    pl.semaphore_wait(barrier, n - 1)

    for h in range(halves):
        some = slice(h * LANES, (h + 1) * LANES)
        product = None
        for k in range(KPARTS):
            if h == 0:
                q_copy(k).wait()
            t_copy(h, k).wait()
            part = slice(k * step, (k + 1) * step)
            term = lax.dot_general(
                q_buf[:, part], t_buf[some, part], DIMS, preferred_element_type=jnp.float32
            )
            product = term if product is None else product + term
        product = product * weights[:, some]
        for d in range(n):
            sbuf[h, d] = product[d * own : (d + 1) * own, :]
        for r in range(1, n):
            where, device = peer(r)
            pltpu.make_async_remote_copy(
                src_ref=sbuf.at[h, where],
                dst_ref=rbuf.at[h, r - 1],
                send_sem=send_sem.at[h],
                recv_sem=recv_sem.at[h],
                device_id=device,
                device_id_type=MESH,
            ).start()

    totals = []
    for h in range(halves):
        landed = rbuf.at[h]
        pltpu.make_async_copy(landed, landed, recv_sem.at[h]).wait()
        total = sbuf[h, me]
        for r in range(1, n):
            total = total + rbuf[h, r - 1]
        totals.append(total)

    for h in range(halves):
        some = slice(h * LANES, (h + 1) * LANES)
        wanted = jnp.broadcast_to(ids[:, some], (own, LANES))
        lane = wanted % LANES
        result = None
        for s in range(halves):
            got = jnp.take_along_axis(totals[s], lane, axis=1, mode="promise_in_bounds")
            result = got if result is None else jnp.where(wanted >= s * LANES, got, result)
        out_ref[:, some] = result

    for h in range(halves):
        gone = sbuf.at[h, pl.ds(0, n - 1)]
        pltpu.make_async_copy(gone, gone, send_sem.at[h]).wait()


def shards(ckpts, wides, query_grads, train_grads, step_rates, layer_mask, train_ids):
    n = ckpts * wides
    _, rows, depth = query_grads.shape
    cols = train_grads.shape[1]
    halves = cols // LANES
    own = rows // n
    return pl.pallas_call(
        functools.partial(kernel, ckpts, wides),
        out_shape=jax.ShapeDtypeStruct((own, cols), jnp.float32),
        in_specs=[
            pl.BlockSpec(memory_space=pltpu.HBM),
        ]
        * 5,
        out_specs=pl.BlockSpec(memory_space=pltpu.VMEM),
        scratch_shapes=[
            pltpu.SMEM(step_rates.shape, jnp.float32),
            pltpu.SMEM(layer_mask.shape, jnp.int32),
            pltpu.VMEM((1, cols), jnp.int32),
            pltpu.VMEM((rows, depth), jnp.bfloat16),
            pltpu.VMEM((cols, depth), jnp.bfloat16),
            pltpu.VMEM((rows, cols), jnp.float32),
            pltpu.VMEM((halves, n, own, LANES), jnp.float32),
            pltpu.VMEM((halves, n - 1, own, LANES), jnp.float32),
            pltpu.SemaphoreType.DMA((3,)),
            pltpu.SemaphoreType.DMA((KPARTS,)),
            pltpu.SemaphoreType.DMA((halves, KPARTS)),
            pltpu.SemaphoreType.DMA((halves,)),
            pltpu.SemaphoreType.DMA((halves,)),
        ],
        compiler_params=pltpu.CompilerParams(
            collective_id=0, has_side_effects=True, vmem_limit_bytes=64 * 1024 * 1024
        ),
        cost_estimate=pl.CostEstimate(
            flops=2 * rows * cols * depth,
            bytes_accessed=2 * (rows + cols) * depth,
            transcendentals=0,
        ),
    )(step_rates, layer_mask, train_ids.reshape(1, cols), query_grads, train_grads)


def solution(mesh):
    in_specs = (
        P("ckpt", "groups", "wide"),
        P("ckpt", "groups", "wide"),
        P("ckpt"),
        P("wide", None, None),
        P(),
    )
    out_specs = P(("groups", "ckpt", "wide"), None)
    body = functools.partial(shards, mesh.shape["ckpt"], mesh.shape["wide"])
    return jax.shard_map(body, mesh=mesh, in_specs=in_specs, out_specs=out_specs, check_vma=False)
```

time: 111 us -> 15.5 us (0.14); the launches traced: 109 us -> 15.3 us
  waiting for transfers between devices: 86.1 us -> 0 us
  between operations: 14.8 us -> 0.66 us
  Pallas kernels: 0 us -> 13.3 us
  matrix products: 4.23 us -> 0 us
  local copies, waits for them, and re-layouts: 2.86 us -> 1.28 us
  other arithmetic: 1.47 us -> 0 us
    unnamed x2 -> x0, waiting for transfers between devices: 86.1 us -> none
    pallas_call x0 -> x1, Pallas kernels: none -> 13.3 us  [shards(): pl.pallas_call(functools.partial(kernel, ckpts, wides), out_shape=jax.Sha...]
    dot_general x2 -> x0, matrix products: 4.23 us -> none  [the longest x1 3.41 us: shards(): lax.dot_general(queries, trained, (((1,), (1,)), ((), ())), preferred_ele...]
  transfers between devices with their start and end apart: 1 -> 0, of which waited for: 1 -> 0; matrix products, arithmetic and copies ran while one was open for 1% -> 0% of each run, Pallas kernels for 0% -> 0%
where the time goes in v1:
time: 15.5 us; the launch traced here: 15.3 us
  Pallas kernels  13.3 us (86%)
  local copies, waits for them, and re-layouts  1.28 us (8%)
  between operations  0.66 us (4%)
    pallas_call x1, Pallas kernels, shards(): pl.pallas_call(functools.partial(kernel, ckpts, wides), out_shape=jax.Sha...  13.3 us
    unnamed x1, local copies, waits for them, and re-layouts  1.28 us

profile of v1, /device:TPU:0, one launch (start us, length us, event | category | flops | bytes accessed | tf_op | source)
XLA Modules:
  0.0 15.3 jit_solution(13811149278044149364)
XLA Ops:
  0.7 13.3 %shard_map.55 = f32[4,256]{1,0:T(4,128)} custom-call(f32[1]{0:T(128)S(6)} %copy.7.rate_hbm, s32[1,4,4]{2,1,0:T(4,128)} %mask_hbm.1, s32[1,256]{1,0:T(1,128)} %bitcast.1, bf16[1,64,8192]{2,1,0:T(8,128)(2,1)} %q_hbm.1, bf16[1,256,8192]{2,1,0:T(8,128)(2,1)} %t_hbm.1), custom_call_target="tpu_custom_call" | custom-call | flops 268435456 | bytes 5242880 | tf_op jit(solution)/shard_map/pallas_call | solution.py:142
  14.0 1.3 %copy.8 = f32[4,256]{1,0:T(4,128)} copy(f32[4,256]{1,0:T(4,128)} %shard_map.55) | data formatting | bytes 8192

commit v2 on v1

v2 whole, which is shorter than its diff:
```python
import functools
import math

import jax
import jax.numpy as jnp
from jax import lax
from jax.experimental import pallas as pl
from jax.experimental.pallas import tpu as pltpu
from jax.sharding import PartitionSpec as P

NQB = 4
NPAN = 4
LANES = 128
SPLITS = (8, 8)
STAGES = (("ckpt", "y", "core"),)
PRIORITY = (0, 0)
MESH = pl.DeviceIdType.MESH
DIMS = (((1,), (1,)), ((), ()))


def bounds(depth):
    total = sum(SPLITS)
    edges = [depth * sum(SPLITS[:k]) // total for k in range(len(SPLITS) + 1)]
    return list(zip(edges[:-1], edges[1:]))


def linear(names, at, sizes):
    place = 0
    for name in names:
        place = place * sizes[name] + at[name]
    return place


def unlinear(names, place, sizes):
    at = {}
    for name in reversed(names):
        at[name] = lax.rem(place, sizes[name])
        place = place // sizes[name]
    return at


def kernel(
    sizes,
    rate_hbm, mask_hbm, ids_hbm, q_hbm, t_hbm, out_ref,
    rate_ref, mask_ref, ids_ref, q_buf, t_buf, weights, *rest,
):
    stages = len(STAGES)
    send_bufs, recv_bufs = rest[:stages], rest[stages : 2 * stages]
    s_sem, q_sem, t_sem, send_sem, recv_sem = rest[2 * stages :]
    n = math.prod(sizes.values())
    rows, depth = q_buf.shape
    cols = t_buf.shape[0]
    own = rows // n
    group = lax.axis_index("groups")
    wide = lax.axis_index("wide")
    at = {"ckpt": lax.axis_index("ckpt"), "y": wide // 2, "core": lax.rem(wide, 2)}

    small = [
        pltpu.make_async_copy(rate_hbm, rate_ref, s_sem.at[0]),
        pltpu.make_async_copy(mask_hbm, mask_ref, s_sem.at[1]),
        pltpu.make_async_copy(ids_hbm, ids_ref, s_sem.at[2]),
    ]
    for copy in small:
        copy.start()
    big = []
    for k, (low, high) in enumerate(bounds(depth)):
        part = pl.ds(low, high - low)
        pair = (
            pltpu.make_async_copy(q_hbm.at[0, :, part], q_buf.at[:, part], q_sem.at[k]),
            pltpu.make_async_copy(t_hbm.at[0, :, part], t_buf.at[:, part], t_sem.at[k]),
        )
        for copy in pair:
            copy.start(priority=PRIORITY[k])
        big.append(pair)

    places, peers = [], []
    for names in STAGES:
        size = math.prod(sizes[name] for name in names)
        place = linear(names, at, sizes)
        places.append(place)
        some = []
        for r in range(1, size):
            there = lax.rem(place + r, size)
            to = {**at, **unlinear(names, there, sizes)}
            some.append((there, (group, to["ckpt"], to["y"] * 2 + to["core"])))
        peers.append(some)

    barrier = pltpu.get_barrier_semaphore()
    for some in peers:
        for _, device in some:
            pl.semaphore_signal(barrier, inc=1, device_id=device, device_id_type=MESH)

    for copy in small:
        copy.wait()
    ids = ids_ref[...]
    hot = (lax.broadcasted_iota(jnp.int32, (cols, cols), 0) == ids).astype(jnp.bfloat16)
    panel = cols // NPAN
    in_panel = (
        lax.broadcasted_iota(jnp.int32, (16, cols), 1) // panel
        == lax.broadcasted_iota(jnp.int32, (16, cols), 0)
    ).astype(jnp.bfloat16)
    stored = lax.dot_general(in_panel, hot, DIMS, preferred_element_type=jnp.float32)
    qblock = rows // NQB
    rate = rate_ref[0]
    for b in range(NQB):
        row = sum(
            (rate * mask_ref[0, b, p].astype(jnp.float32)) * stored[p : p + 1, :]
            for p in range(NPAN)
        )
        weights[b * qblock : (b + 1) * qblock, :] = jnp.broadcast_to(row, (qblock, cols))

    product = None
    for (low, high), pair in zip(bounds(depth), big):
        for copy in pair:
            copy.wait()
        term = lax.dot_general(
            t_buf[:, low:high], q_buf[:, low:high], DIMS, preferred_element_type=jnp.float32
        )
        product = term if product is None else product + term
    product = product.T * weights[...]

    for d in range(n):
        where = {"ckpt": d // (sizes["y"] * 2), "y": d // 2 % sizes["y"], "core": d % 2}
        order = [name for names in STAGES for name in names]
        send_bufs[0][linear(order, where, sizes)] = product[d * own : (d + 1) * own, :]

    pl.semaphore_wait(barrier, sum(len(some) for some in peers))

    left = n
    total = None
    for s, some in enumerate(peers):
        left = left // (len(some) + 1)
        for r, (there, device) in enumerate(some):
            pltpu.make_async_remote_copy(
                src_ref=send_bufs[s].at[pl.ds(there * left, left)],
                dst_ref=recv_bufs[s].at[pl.ds(r * left, left)],
                send_sem=send_sem.at[s],
                recv_sem=recv_sem.at[s],
                device_id=device,
                device_id_type=MESH,
            ).start()
        total = send_bufs[s][pl.ds(places[s] * left, left)]
        pltpu.make_async_copy(recv_bufs[s], recv_bufs[s], recv_sem.at[s]).wait()
        for r in range(len(some)):
            total = total + recv_bufs[s][r * left : (r + 1) * left]
        if s + 1 < stages:
            send_bufs[s + 1][...] = total
    total = total[0]

    halves = cols // LANES
    for h in range(halves):
        some = slice(h * LANES, (h + 1) * LANES)
        wanted = jnp.broadcast_to(ids[:, some], (own, LANES))
        lane = wanted % LANES
        result = None
        for s in range(halves):
            part = total[:, s * LANES : (s + 1) * LANES]
            got = jnp.take_along_axis(part, lane, axis=1, mode="promise_in_bounds")
            result = got if result is None else jnp.where(wanted >= s * LANES, got, result)
        out_ref[:, some] = result

    for s in range(stages):
        gone = recv_bufs[s]
        pltpu.make_async_copy(gone, gone, send_sem.at[s]).wait()


def shards(sizes, query_grads, train_grads, step_rates, layer_mask, train_ids):
    n = math.prod(sizes.values())
    _, rows, depth = query_grads.shape
    cols = train_grads.shape[1]
    own = rows // n
    send_shapes, recv_shapes, left = [], [], n
    for names in STAGES:
        size = math.prod(sizes[name] for name in names)
        send_shapes.append((left, own, cols))
        recv_shapes.append((left - left // size, own, cols))
        left = left // size
    in_hbm = [
        pltpu.with_memory_space_constraint(x, pltpu.HBM)
        for x in (layer_mask, train_ids.reshape(1, cols), query_grads, train_grads)
    ]
    return pl.pallas_call(
        functools.partial(kernel, sizes),
        out_shape=jax.ShapeDtypeStruct((own, cols), jnp.float32),
        in_specs=[pl.BlockSpec(memory_space=pltpu.HBM)] * 5,
        out_specs=pl.BlockSpec(memory_space=pltpu.VMEM),
        scratch_shapes=[
            pltpu.SMEM(step_rates.shape, jnp.float32),
            pltpu.SMEM(layer_mask.shape, jnp.int32),
            pltpu.VMEM((1, cols), jnp.int32),
            pltpu.VMEM((rows, depth), jnp.bfloat16),
            pltpu.VMEM((cols, depth), jnp.bfloat16),
            pltpu.VMEM((rows, cols), jnp.float32),
            *[pltpu.VMEM(shape, jnp.float32) for shape in send_shapes],
            *[pltpu.VMEM(shape, jnp.float32) for shape in recv_shapes],
            pltpu.SemaphoreType.DMA((3,)),
            pltpu.SemaphoreType.DMA((len(SPLITS),)),
            pltpu.SemaphoreType.DMA((len(SPLITS),)),
            pltpu.SemaphoreType.DMA((len(STAGES),)),
            pltpu.SemaphoreType.DMA((len(STAGES),)),
        ],
        compiler_params=pltpu.CompilerParams(
            collective_id=0, has_side_effects=True, vmem_limit_bytes=48 * 1024 * 1024
        ),
        cost_estimate=pl.CostEstimate(
            flops=2 * rows * cols * depth,
            bytes_accessed=2 * (rows + cols) * depth,
            transcendentals=0,
        ),
    )(step_rates, *in_hbm)


def solution(mesh):
    in_specs = (
        P("ckpt", "groups", "wide"),
        P("ckpt", "groups", "wide"),
        P("ckpt"),
        P("wide", None, None),
        P(),
    )
    out_specs = P(("groups", "ckpt", "wide"), None)
    sizes = {"ckpt": mesh.shape["ckpt"], "y": mesh.shape["wide"] // 2, "core": 2}
    body = functools.partial(shards, sizes)
    return jax.shard_map(body, mesh=mesh, in_specs=in_specs, out_specs=out_specs, check_vma=False)
```

time: 15.5 us -> 13.1 us (0.85)
  Pallas kernels: 13.3 us -> 11.7 us
  local copies, waits for them, and re-layouts: 1.28 us -> 0.6 us
    pallas_call x1, Pallas kernels: 13.3 us -> 11.7 us  [shards(): pl.pallas_call(functools.partial(kernel, sizes), out_shape=jax.ShapeDtype...]
    unnamed x1, local copies, waits for them, and re-layouts: 1.28 us -> 0.6 us
where the time goes in v2:
time: 13.1 us; the launch traced here: 12.9 us
  Pallas kernels  11.7 us (89%)
  between operations  0.66 us (5%)
  local copies, waits for them, and re-layouts  0.6 us (5%)
    pallas_call x1, Pallas kernels, shards(): pl.pallas_call(functools.partial(kernel, sizes), out_shape=jax.ShapeDtype...  11.7 us
    unnamed x1, local copies, waits for them, and re-layouts  0.6 us

profile of v2, /device:TPU:0, one launch (start us, length us, event | category | flops | bytes accessed | tf_op | source)
XLA Modules:
  0.0 12.9 jit_solution(1606742350255198011)
XLA Ops:
  0.7 11.7 %shard_map.55 = f32[4,256]{1,0:T(4,128)S(1)} custom-call(f32[1]{0:T(128)S(6)} %copy.7.rate_hbm, s32[1,4,4]{2,1,0:T(4,128)} %mask_hbm.1, s32[1,256]{1,0:T(1,128)} %bitcast.1, bf16[1,64,8192]{2,1,0:T(8,128)(2,1)} %q_hbm.1, bf16[1,256,8192]{2,1,0:T(8,128)(2,1)} %t_hbm.1), custom_call_target="tpu_custom_call" | custom-call | flops 268435456 | bytes 5242880 | tf_op jit(solution)/shard_map/pallas_call | solution.py:182
  12.3 0.6 %copy.8 = f32[4,256]{1,0:T(4,128)} copy(f32[4,256]{1,0:T(4,128)S(1)} %shard_map.55) | data formatting | bytes 8192
